TPU v7x, 32 devices: a whole 2x2x4 slice. The times are simulated.
32 devices in a mesh: tp: 4 (over y, x), dp: 8 (over z, core).
Axes of the slice: x: 2, y: 2, z: 4, core: 2. Of those that a mesh axis runs over, the one named last changes fastest.
Arguments:
- tokens: bfloat16 [8, 1024, 1152], P('dp', 'tp'), may hold values from -6 to 6
- condition: bfloat16 [16, 1152], P('dp'), may hold values from -6 to 6
- modulator: bfloat16 [1152, 6, 1152], P(None, None, 'tp'), may hold values from -0.1875 to 0.1875
- offsets: float32 [6, 1152], replicated, may hold values from -3 to 3
- inward: bfloat16 [1152, 3, 1152], P(None, None, 'tp'), may hold values from -0.1875 to 0.1875
- query_gain: float32 [72], replicated, may hold values from 0.1 to 1.9
- key_gain: float32 [72], replicated, may hold values from 0.1 to 1.9
- outward: bfloat16 [1152, 1152], P(None, 'tp'), may hold values from -1 to 1
- expansion: bfloat16 [1152, 2, 3072], P(None, None, 'tp'), may hold values from -0.1875 to 0.1875
- contraction: bfloat16 [1152, 3072], P(None, 'tp'), may hold values from -0.109375 to 0.109375
- item_lengths: int32 [8, 4], P('dp'), may hold values from 1 to 832, 1024 in all within a row
- item_condition: int32 [8, 4], P('dp'), may hold values from 0 to 1
- patch_rows: int32 [8, 1024], P('dp'), may hold values from 0 to 63
- patch_columns: int32 [8, 1024], P('dp'), may hold values from 0 to 63
- cotangent: bfloat16 [8, 1024, 1152], P('dp', 'tp'), may hold values from -6 to 6
Outputs:
- layer_output: bfloat16 [8, 1024, 1152], P('dp', 'tp')
- token_gradient: float32 [8, 1024, 1152], P('dp', 'tp')
- modulator_gradient: float32 [1152, 6, 1152], P('dp', None, 'tp')
- bias_gradient: float32 [6, 1152], replicated
- inward_gradient: float32 [1152, 3, 1152], P('dp', None, 'tp')
- query_gradient: float32 [72], replicated
- key_gradient: float32 [72], replicated
- outward_gradient: float32 [1152, 1152], P('dp', 'tp')
- expansion_gradient: float32 [1152, 2, 3072], P('dp', None, 'tp')
- contraction_gradient: float32 [1152, 3072], P('dp', 'tp')
Inputs may be any that keep to these rules, and one draw needn't show every extreme that they name: `item_lengths`: the 4 lengths of each sequence sum to 1024; the largest of each sequence is exactly 832.
All inputs are finite; a program needn't handle non-finite values.
Results may differ from a plain program's by a relative error of at most 0.017.
Values may be sent and summed in bfloat16 or wider, within the bound.
No kernel may reach another device: no remote copies, remote signals or barrier semaphores. Data moves between devices by JAX's collectives and lax.ppermute only.
A program may use at most 192 MiB of HBM per device.

v0:
```python
import math

import jax
import jax.numpy as jnp
from jax import lax
from jax.sharding import PartitionSpec as P


def layer_norm(values):
    center = values - jnp.mean(values, axis=-1, keepdims=True)
    variance = jnp.mean(center * center, axis=-1, keepdims=True)
    return center * lax.rsqrt(variance + 1e-06)


def modulate(values, shift, scaling):
    return layer_norm(values) * (1.0 + scaling) + shift


def rope_tables(patch_rows, patch_columns, head_dim):
    quarter = head_dim // 4
    frequency = 10000.0 ** (-jnp.arange(quarter, dtype=jnp.float32) / quarter)
    along_rows = patch_rows.astype(jnp.float32)[..., None] * frequency
    along_columns = patch_columns.astype(jnp.float32)[..., None] * frequency
    angles = jnp.concatenate([along_rows, along_rows, along_columns, along_columns], axis=-1)
    return (jnp.cos(angles), jnp.sin(angles))


def turn_half(values):
    quarter = values.shape[-1] // 4
    part_one = values[..., :quarter]
    part_two = values[..., quarter : 2 * quarter]
    part_three = values[..., 2 * quarter : 3 * quarter]
    part_four = values[..., 3 * quarter :]
    return jnp.concatenate([-part_two, part_one, -part_four, part_three], axis=-1)


def prepare(projected_rows, scaling, cosine, sine_table):
    normed = (
        projected_rows
        * lax.rsqrt(jnp.mean(projected_rows * projected_rows, axis=-1, keepdims=True) + 1e-06)
        * scaling
    )
    return normed * cosine + turn_half(normed) * sine_table


def item_number(lengths, full_len):
    item_ends = jnp.cumsum(lengths, axis=-1)
    positions = jnp.arange(full_len, dtype=jnp.int32)
    return jnp.sum((positions[None, :, None] >= item_ends[:, None, :]).astype(jnp.int32), axis=-1)


def masked_scores(queries, key_rows, owning_sequences):
    factor = 1.0 / math.sqrt(queries.shape[-1])
    scores = (
        jnp.einsum("qhe,khe->hqk", queries, key_rows, preferred_element_type=jnp.float32) * factor
    )
    same_item = (owning_sequences[:, None] == owning_sequences[None, :])[None]
    return jnp.where(same_item, scores, -1e30)


def attend_forward(queries, key_rows, values, owning_sequences):
    scores = masked_scores(queries, key_rows, owning_sequences)
    row_top = jnp.max(scores, axis=-1, keepdims=True)
    weights = jnp.exp(scores - row_top)
    row_total = jnp.sum(weights, axis=-1, keepdims=True)
    rounded = (weights / row_total).astype(jnp.bfloat16)
    mixed = jnp.einsum("hqk,khe->qhe", rounded, values, preferred_element_type=jnp.float32)
    return (mixed, (row_top + jnp.log(row_total))[..., 0])


def attend_backward(queries, key_rows, values, owning_sequences, log_total, mixed_grad):
    factor = 1.0 / math.sqrt(queries.shape[-1])
    scores = masked_scores(queries, key_rows, owning_sequences)
    weights = jnp.exp(scores - log_total[..., None])
    value_grad = jnp.einsum(
        "hqk,qhe->khe", weights.astype(jnp.bfloat16), mixed_grad, preferred_element_type=jnp.float32
    )
    weight_grad = jnp.einsum("qhe,khe->hqk", mixed_grad, values, preferred_element_type=jnp.float32)
    centre = jnp.sum(weights * weight_grad, axis=-1, keepdims=True)
    score_grad = (weights * (weight_grad - centre)).astype(jnp.bfloat16)
    query_grad = (
        jnp.einsum("hqk,khe->qhe", score_grad, key_rows, preferred_element_type=jnp.float32)
        * factor
    )
    key_grad = (
        jnp.einsum("hqk,qhe->khe", score_grad, queries, preferred_element_type=jnp.float32) * factor
    )
    return (query_grad, key_grad, value_grad)


def shards(
    tokens,
    condition,
    modulator,
    offsets,
    inward,
    query_gain,
    key_gain,
    outward,
    expansion,
    contraction,
    item_lengths,
    item_condition,
    patch_rows,
    patch_columns,
    cotangent,
):
    seq_count, local_len, width = tokens.shape
    full_len = patch_rows.shape[1]
    head_dim = query_gain.shape[0]
    local_heads = inward.shape[2] // head_dim
    cond_count = condition.shape[0]
    exact = lax.Precision.HIGHEST
    owning_sequences = item_number(item_lengths, full_len)
    first_row = lax.axis_index("tp") * local_len
    local_owners = lax.dynamic_slice_in_dim(owning_sequences, first_row, local_len, 1)
    item_hot = (
        local_owners[:, :, None] == jnp.arange(item_lengths.shape[1], dtype=jnp.int32)
    ).astype(jnp.int32)
    token_cond = jnp.sum(item_hot * item_condition[:, None, :], axis=-1)
    cond_hot = (token_cond[:, :, None] == jnp.arange(cond_count, dtype=jnp.int32)).astype(
        jnp.float32
    )
    cond_low = jax.nn.silu(condition.astype(jnp.float32)).astype(jnp.bfloat16)
    local_shares = jnp.einsum(
        "cd,dje->cje", cond_low, modulator, preferred_element_type=jnp.float32
    )
    portion_shares = lax.all_gather(local_shares, "tp", axis=2, tiled=True) + offsets
    per_token = jnp.einsum("slc,cjd->sljd", cond_hot, portion_shares, precision=exact)
    shift_one, scale_one, gate_one, shift_two, scale_two, gate_two = [
        per_token[:, :, column] for column in range(6)
    ]
    cosine, sine_table = rope_tables(patch_rows, patch_columns, head_dim)
    cosine = cosine[:, :, None, :]
    sine_table = sine_table[:, :, None, :]
    head_shape = (seq_count, full_len, local_heads, head_dim)
    stream = tokens.astype(jnp.float32)
    first_in = modulate(stream, shift_one, scale_one).astype(jnp.bfloat16)
    first_gathered = lax.all_gather(first_in, "tp", axis=1, tiled=True)
    projected_rows = jnp.einsum(
        "ocn,nub->ocub", first_gathered, inward, preferred_element_type=jnp.float32
    )
    query_raw = projected_rows[:, :, 0].reshape(head_shape)
    key_raw = projected_rows[:, :, 1].reshape(head_shape)
    queries = prepare(query_raw, query_gain, cosine, sine_table).astype(jnp.bfloat16)
    key_rows = prepare(key_raw, key_gain, cosine, sine_table).astype(jnp.bfloat16)
    values = projected_rows[:, :, 2].reshape(head_shape).astype(jnp.bfloat16)
    mixed, log_total = lax.map(
        lambda parts: attend_forward(*parts), (queries, key_rows, values, owning_sequences)
    )
    mixed_low = mixed.reshape(seq_count, full_len, -1).astype(jnp.bfloat16)
    attended = lax.psum_scatter(
        jnp.einsum("sli,oi->slo", mixed_low, outward, preferred_element_type=jnp.float32),
        "tp",
        scatter_dimension=1,
        tiled=True,
    )
    middle = stream + gate_one * attended
    second_in = modulate(middle, shift_two, scale_two).astype(jnp.bfloat16)
    second_gathered = lax.all_gather(second_in, "tp", axis=1, tiled=True)
    gate_lifting_pair = jnp.einsum(
        "omz,zhq->omhq", second_gathered, expansion, preferred_element_type=jnp.float32
    )
    gate_part = gate_lifting_pair[:, :, 0]
    up_part = gate_lifting_pair[:, :, 1]
    activated = jax.nn.silu(gate_part)
    hidden = (activated * up_part).astype(jnp.bfloat16)
    fed = lax.psum_scatter(
        jnp.einsum("slf,of->slo", hidden, contraction, preferred_element_type=jnp.float32).astype(
            jnp.bfloat16
        ),
        "tp",
        scatter_dimension=1,
        tiled=True,
    ).astype(jnp.float32)
    layer_output = (middle + gate_two * fed).astype(jnp.bfloat16)
    upstream = cotangent.astype(jnp.float32)
    gate_two_grad = upstream * fed
    fed_all = lax.all_gather((gate_two * upstream).astype(jnp.bfloat16), "tp", axis=1, tiled=True)
    hidden_grad = jnp.einsum(
        "slo,of->slf", fed_all, contraction, preferred_element_type=jnp.float32
    )
    contraction_grad = jnp.einsum(
        "slo,slf->of", fed_all, hidden, preferred_element_type=jnp.float32
    )
    sigmoid = jax.nn.sigmoid(gate_part)
    gate_grad = hidden_grad * up_part * (sigmoid + activated * (1.0 - sigmoid))
    up_grad = hidden_grad * activated
    widening_gradient = jnp.stack([gate_grad, up_grad], axis=2).astype(jnp.bfloat16)
    expansion_grad = jnp.einsum(
        "ypu,ypwz->uwz", second_gathered, widening_gradient, preferred_element_type=jnp.float32
    )
    second_grad = lax.psum_scatter(
        jnp.einsum(
            "nukr,vkr->nuv", widening_gradient, expansion, preferred_element_type=jnp.float32
        ).astype(jnp.bfloat16),
        "tp",
        scatter_dimension=1,
        tiled=True,
    ).astype(jnp.float32)
    unused_two, pull_two = jax.vjp(modulate, middle, shift_two, scale_two)
    middle_norm_grad, shift_two_grad, scale_two_grad = pull_two(second_grad)
    middle_grad = upstream + middle_norm_grad
    gate_one_grad = middle_grad * attended
    attended_all = lax.all_gather(
        (gate_one * middle_grad).astype(jnp.bfloat16), "tp", axis=1, tiled=True
    )
    mixed_grad = jnp.einsum(
        "slo,oi->sli", attended_all, outward, preferred_element_type=jnp.float32
    ).astype(jnp.bfloat16)
    outward_grad = jnp.einsum(
        "slo,sli->oi", attended_all, mixed_low, preferred_element_type=jnp.float32
    )
    mixed_grad = mixed_grad.reshape(head_shape)
    query_grad, key_grad, value_grad = lax.map(
        lambda parts: attend_backward(*parts),
        (queries, key_rows, values, owning_sequences, log_total, mixed_grad),
    )

    def both_heads(query_in, key_in, query_scale, key_scale):
        return (
            prepare(query_in, query_scale, cosine, sine_table),
            prepare(key_in, key_scale, cosine, sine_table),
        )

    unused_heads, pull_heads = jax.vjp(both_heads, query_raw, key_raw, query_gain, key_gain)
    query_raw_grad, key_raw_grad, query_scale_grad, key_scale_grad = pull_heads(
        (query_grad, key_grad)
    )
    projected_rows_gradient = jnp.stack([query_raw_grad, key_raw_grad, value_grad], axis=2)
    projected_rows_gradient = projected_rows_gradient.reshape(seq_count, full_len, 3, -1).astype(
        jnp.bfloat16
    )
    inward_grad = jnp.einsum(
        "qyc,qyru->cru", first_gathered, projected_rows_gradient, preferred_element_type=jnp.float32
    )
    first_grad = lax.psum_scatter(
        jnp.einsum(
            "tqkf,ckf->tqc", projected_rows_gradient, inward, preferred_element_type=jnp.float32
        ).astype(jnp.bfloat16),
        "tp",
        scatter_dimension=1,
        tiled=True,
    ).astype(jnp.float32)
    unused_one, pull_one = jax.vjp(modulate, stream, shift_one, scale_one)
    stream_norm_grad, shift_one_grad, scale_one_grad = pull_one(first_grad)
    token_gradient = middle_grad + stream_norm_grad
    token_mod_grad = jnp.stack(
        [
            shift_one_grad,
            scale_one_grad,
            gate_one_grad,
            shift_two_grad,
            scale_two_grad,
            gate_two_grad,
        ],
        axis=2,
    )
    slot_grad = jnp.einsum("slc,sljd->cjd", cond_hot, token_mod_grad, precision=exact)
    slot_share = lax.psum_scatter(
        slot_grad.astype(jnp.bfloat16), "tp", scatter_dimension=2, tiled=True
    ).astype(jnp.float32)
    modulator_grad = jnp.einsum(
        "cd,cje->dje", cond_low.astype(jnp.float32), slot_share, precision=exact
    )
    query_gradient, key_gradient, bias_gradient = lax.psum(
        (query_scale_grad, key_scale_grad, jnp.sum(slot_grad, axis=0)), ("tp", "dp")
    )
    inward_grad, outward_grad, expansion_grad, contraction_grad, modulator_grad = (
        lax.psum_scatter(inward_grad, "dp", scatter_dimension=0, tiled=True),
        lax.psum_scatter(outward_grad, "dp", scatter_dimension=0, tiled=True),
        lax.psum_scatter(expansion_grad, "dp", scatter_dimension=0, tiled=True),
        lax.psum_scatter(contraction_grad, "dp", scatter_dimension=0, tiled=True),
        lax.psum_scatter(modulator_grad, "dp", scatter_dimension=0, tiled=True),
    )
    return (
        layer_output,
        token_gradient,
        modulator_grad,
        bias_gradient,
        inward_grad,
        query_gradient,
        key_gradient,
        outward_grad,
        expansion_grad,
        contraction_grad,
    )


def solution(mesh):
    placed = (
        P("dp", "tp", None),
        P("dp", None),
        P(None, None, "tp"),
        P(),
        P(None, None, "tp"),
        P(),
        P(),
        P(None, "tp"),
        P(None, None, "tp"),
        P(None, "tp"),
        P("dp", None),
        P("dp", None),
        P("dp", None),
        P("dp", None),
        P("dp", "tp", None),
    )
    return jax.shard_map(
        shards,
        mesh=mesh,
        in_specs=placed,
        out_specs=(
            P("dp", "tp", None),
            P("dp", "tp", None),
            P("dp", None, "tp"),
            P(),
            P("dp", None, "tp"),
            P(),
            P(),
            P("dp", "tp"),
            P("dp", None, "tp"),
            P("dp", "tp"),
        ),
        check_vma=False,
    )
```

profile of v0, /device:TPU:0, one launch (start us, length us, event | category | flops | bytes accessed | tf_op | source)
XLA Modules:
  0.0 870.4 jit_solution(11445057557451303454)
XLA Ops:
  19.6 17.1 %all_gather.15 = f32[2,6,1152]{1,0,2:T(2,128)S(1)} all-gather(f32[2,6,288]{1,0,2:T(2,128)} %copy.45), channel_id=1, replica_groups=mesh['tp'=4,'dp'=8] {'tp'}, dimensions={2}, use_global_device_ids=true | all-gather | bytes 69120 | tf_op jit(solution)/shard_map/all_gather | solution.py:128
  52.9 33.9 %all-gather.5.cloned.1.call-done = bf16[1,1024,1152]{2,1,0:T(8,128)(2,1)} async-done(((bf16[1,256,1152]{2,1,0:T(8,128)(2,1)}), bf16[1,1024,1152]{2,1,0:T(8,128)(2,1)}) %all-gather.5.cloned.1.call-update) | async-done | bytes 2359312 | tf_op jit(solution)/shard_map/all_gather | solution.py:139
  86.8 4.7 fusion.38
  96.2 7.5 fusion.122
  103.7 8.0 fusion
  111.8 7.9 fusion.56
  124.2 57.2 %reduce-scatter.13.cloned.1.call-done = f32[1,256,1152]{2,1,0:T(8,128)} async-done(((f32[1,1024,1152]{2,1,0:T(8,128)}), f32[1,256,1152]{2,1,0:T(8,128)}) %reduce-scatter.13.cloned.1.call-update) | async-done | bytes 1179664 | tf_op jit(solution)/shard_map/reduce_scatter | solution.py:152
  188.9 37.0 %all-gather.7.cloned.1.call-done = bf16[1,1024,1152]{2,1,0:T(8,128)(2,1)} async-done(((bf16[1,256,1152]{2,1,0:T(8,128)(2,1)}), bf16[1,1024,1152]{2,1,0:T(8,128)(2,1)}) %all-gather.7.cloned.1.call-update) | async-done | bytes 2359312 | tf_op jit(solution)/shard_map/all_gather | solution.py:160
  225.9 7.9 fusion.20
  233.8 31.9 %all-gather.9.cloned.1.call-done = bf16[1,1024,1152]{2,1,0:T(8,128)(2,1)} async-done(((bf16[1,256,1152]{2,1,0:T(8,128)(2,1)}), bf16[1,1024,1152]{2,1,0:T(8,128)(2,1)}) %all-gather.9.cloned.1.call-update) | async-done | bytes 2359312 | tf_op jit(solution)/shard_map/all_gather | solution.py:179
  265.7 6.8 fusion.46
  274.2 5.5 fusion.9
  281.2 6.9 fusion.8
  288.3 29.1 %reduce-scatter.17.cloned.1.call-done = bf16[1,256,1152]{2,1,0:T(8,128)(2,1)} async-done(((bf16[1,1024,1152]{2,1,0:T(8,128)(2,1)}), bf16[1,256,1152]{2,1,0:T(8,128)(2,1)}) %reduce-scatter.17.cloned.1.call-update) | async-done | bytes 589840 | tf_op jit(solution)/shard_map/reduce_scatter | solution.py:193
  319.7 37.9 %reduce-scatter.15.cloned.1.call-done = bf16[1,256,1152]{2,1,0:T(8,128)(2,1)} async-done(((bf16[1,1024,1152]{2,1,0:T(8,128)(2,1)}), bf16[1,256,1152]{2,1,0:T(8,128)(2,1)}) %reduce-scatter.15.cloned.1.call-update) | async-done | bytes 589840 | tf_op jit(solution)/shard_map/reduce_scatter | solution.py:168
  363.9 37.4 %all-gather.11.cloned.1.call-done = bf16[1,1024,1152]{2,1,0:T(8,128)(2,1)} async-done(((bf16[1,256,1152]{2,1,0:T(8,128)(2,1)}), bf16[1,1024,1152]{2,1,0:T(8,128)(2,1)}) %all-gather.11.cloned.1.call-update) | async-done | bytes 2359312 | tf_op jit(solution)/shard_map/all_gather | solution.py:205
  404.0 8.5 fusion.53
  412.6 10.9 %multiply_reduce_fusion = (f32[4,1024]{1,0:T(4,128)S(1)}, f32[4,1024,1024]{1,2,0:T(8,128)}) fusion(f32[4,1024,1024]{1,2,0:T(8,128)} %get-tuple-element.145, f32[4,1024]{1,0:T(4,128)S(1)} %log_add_fusion, bf16[1024,4,72]{0,2,1:T(8,128)(2,1)S(1)} %bitcast.265, bf16[1024,4,72]{0,2,1:T(8,128)(2,1)S(1)} %bitcast.267), kind=kOutput, calls=%fused_computation.1 | convolution fusion | flops 616558592 | bytes 34766848 | tf_op jit(solution)/shard_map/while/body/eval_jaxpr/qhe,khe->hqk/dot_general | solution.py:78
  423.5 11.8 %multiply_convert_fusion = bf16[4,1024,1024]{1,2,0:T(8,128)(2,1)S(1)} fusion(f32[4,1024,1024]{1,2,0:T(8,128)} %get-tuple-element.147, f32[4,1024,1024]{1,2,0:T(8,128)} %get-tuple-element.145, f32[4,1024]{1,0:T(4,128)S(1)} %get-tuple-element.146, f32[4,1024]{1,0:T(4,128)S(1)} %log_add_fusion), kind=kLoop, calls=%fused_computation | loop fusion | flops 16777216 | bytes 41975808 | tf_op jit(solution)/shard_map/while/body/eval_jaxpr/convert_element_type | solution.py:80
  446.6 4.1 fusion.10
  451.0 37.3 %reduce-scatter.19.cloned.1.call-done = bf16[1,256,1152]{2,1,0:T(8,128)(2,1)} async-done(((bf16[1,1024,1152]{2,1,0:T(8,128)(2,1)}), bf16[1,256,1152]{2,1,0:T(8,128)(2,1)}) %reduce-scatter.19.cloned.1.call-update) | async-done | bytes 589840 | tf_op jit(solution)/shard_map/reduce_scatter | solution.py:237
  503.7 9.4 %fusion.31 = f32[1152,2,768]{2,0,1:T(8,128)} fusion(bf16[1,1024,1152]{2,1,0:T(8,128)(2,1)} %all-gather.7.cloned.1.call-done, bf16[1024,1,768]{2,0,1:T(8,128)(2,1)} %copy-done.86, bf16[1024,1,768]{2,0,1:T(8,128)(2,1)} %copy-done.85), kind=kOutput, calls=%fused_computation.46 | convolution fusion | flops 3630170112 | bytes 12582912 | tf_op jit(solution)/shard_map/ypu,ypwz->uwz/dot_general | solution.py:190
  513.2 7.6 fusion.27
  521.8 4.3 fusion.23
  527.6 7.3 fusion.34
  536.2 5.7 fusion.82
  542.6 42.0 %all-reduce.8 = (f32[6,1152]{1,0:T(8,128)}, f32[72]{0:T(128)}, f32[72]{0:T(128)}) all-reduce(f32[6,1152]{1,0:T(8,128)S(1)} %get-tuple-element.140, f32[72]{0:T(128)S(1)} %copy-done.76, f32[72]{0:T(128)S(1)} %copy-done.77), channel_id=1, replica_groups=mesh['tp'=4,'dp'=8] {'tp','dp'}, use_global_device_ids=true, to_apply=%region_25.26 | all-reduce | flops 7056 | bytes 56448 | tf_op jit(solution)/shard_map/psum | solution.py:266
  589.6 19.0 %reduce-scatter.27.cloned.1.call-done = f32[144,2,768]{2,0,1:T(8,128)} async-done(((f32[1152,2,768]{2,0,1:T(8,128)}), f32[144,2,768]{2,0,1:T(8,128)}) %reduce-scatter.27.cloned.1.call-update) | async-done | bytes 884752 | tf_op jit(solution)/shard_map/reduce_scatter | solution.py:272
  611.3 42.4 %reduce-scatter.29.cloned.1.call-done = f32[144,768]{1,0:T(8,128)} async-done(((f32[1152,768]{1,0:T(8,128)}), f32[144,768]{1,0:T(8,128)}) %reduce-scatter.29.cloned.1.call-update) | async-done | bytes 442384 | tf_op jit(solution)/shard_map/reduce_scatter | solution.py:273
  653.6 36.3 %reduce-scatter.25.cloned.1.call-done = f32[144,288]{1,0:T(8,128)} async-done(((f32[1152,288]{1,0:T(8,128)}), f32[144,288]{1,0:T(8,128)}) %reduce-scatter.25.cloned.1.call-update) | async-done | bytes 165904 | tf_op jit(solution)/shard_map/reduce_scatter | solution.py:271
  689.9 61.7 %reduce-scatter.23.cloned.1.call-done = f32[144,3,288]{2,0,1:T(8,128)} async-done(((f32[1152,3,288]{2,0,1:T(8,128)}), f32[144,3,288]{2,0,1:T(8,128)}) %reduce-scatter.23.cloned.1.call-update) | async-done | bytes 497680 | tf_op jit(solution)/shard_map/reduce_scatter | solution.py:270
  751.6 111.9 %reduce-scatter.21.cloned.1.call-done = f32[144,6,288]{2,0,1:T(8,128)} async-done(((f32[1152,6,288]{2,0,1:T(8,128)}), f32[144,6,288]{2,0,1:T(8,128)}) %reduce-scatter.21.cloned.1.call-update) | async-done | bytes 995344 | tf_op jit(solution)/shard_map/reduce_scatter | solution.py:274
  (273 shorter events, 98.1 us)
Async XLA Ops:
  7.2 218.8 %copy-start = (bf16[1152,2,768]{2,1,0:T(2,128)(2,1)S(1)}, bf16[1152,2,768]{2,1,0:T(2,128)(2,1)}, u32[]{:S(2)}) copy-start(bf16[1152,2,768]{2,1,0:T(2,128)(2,1)} %param.23) | copy-start | bytes 10616836
  7.2 79.6 %all-gather.5.cloned.1.call-start = ((), (), s32[]{:S(2)}) async-start(), calls=%async_computation.10 | async-start | bytes 2949120 | tf_op jit(solution)/shard_map/all_gather | solution.py:139
  10.0 34.9 %copy-start.54 = (f32[256]{0:T(256)}, f32[256]{0:T(256)S(1)}, u32[]{:S(2)}) copy-start(f32[256]{0:T(256)S(1)} %broadcast_multiply_fusion.5) | copy-start | bytes 3076
  19.6 17.1 %copy-start.27 = (f32[6,1152]{0,1:T(8,128)S(1)}, f32[6,1152]{0,1:T(8,128)}, u32[]{:S(2)}) copy-start(f32[6,1152]{0,1:T(8,128)} %copy.46) | copy-start | bytes 82948
  48.9 132.5 %reduce-scatter.13.cloned.1.call-start = ((), (), s32[]{:S(2)}) async-start(), calls=%async_computation.11 | async-start | bytes 5898240 | tf_op jit(solution)/shard_map/reduce_scatter | solution.py:152
  91.7 20.1 %copy-start.29 = (bf16[1,1024,1,288]{1,3,2,0:T(8,128)(2,1)}, bf16[1,1024,1,288]{1,3,2,0:T(8,128)(2,1)S(1)}, u32[]{:S(2)}) copy-start(bf16[1,1024,1,288]{1,3,2,0:T(8,128)(2,1)S(1)} %slice.182) | copy-start | bytes 1769476
  111.8 8.7 %copy-start.82 = (bf16[1152,288]{0,1:T(8,128)(2,1)S(1)}, bf16[1152,288]{0,1:T(8,128)(2,1)}, u32[]{:S(2)}) copy-start(bf16[1152,288]{0,1:T(8,128)(2,1)} %param.22) | copy-start | bytes 1990660
  124.2 101.7 %all-gather.7.cloned.1.call-start = ((), (), s32[]{:S(2)}) async-start(), calls=%async_computation.12 | async-start | bytes 2949120 | tf_op jit(solution)/shard_map/all_gather | solution.py:160
  188.3 77.4 %all-gather.9.cloned.1.call-start = ((), (), s32[]{:S(2)}) async-start(), calls=%async_computation.14 | async-start | bytes 2949120 | tf_op jit(solution)/shard_map/all_gather | solution.py:179
  188.9 128.4 %reduce-scatter.17.cloned.1.call-start = ((), (), s32[]{:S(2)}) async-start(), calls=%async_computation.15 | async-start | bytes 2949120 | tf_op jit(solution)/shard_map/reduce_scatter | solution.py:193
  279.8 77.9 %reduce-scatter.15.cloned.1.call-start = ((), (), s32[]{:S(2)}) async-start(), calls=%async_computation.13 | async-start | bytes 2949120 | tf_op jit(solution)/shard_map/reduce_scatter | solution.py:168
  288.2 29.2 %copy-start.4 = (f32[1,256,1152]{2,1,0:T(8,128)S(1)}, f32[1,256,1152]{2,1,0:T(8,128)}, u32[]{:S(2)}) copy-start(f32[1,256,1152]{2,1,0:T(8,128)} %copy-done.3) | copy-start | bytes 3538948
  288.2 29.2 %copy-start.52 = (f32[256]{0:T(256)S(1)}, f32[256]{0:T(256)}, u32[]{:S(2)}) copy-start(f32[256]{0:T(256)} %copy-done.51) | copy-start | bytes 3076
  288.2 30.9 %copy-start.67 = (f32[256]{0:T(256)S(1)}, f32[256]{0:T(256)}, u32[]{:S(2)}) copy-start(f32[256]{0:T(256)} %copy-done.66) | copy-start | bytes 3076
  288.2 113.0 %all-gather.11.cloned.1.call-start = ((), (), s32[]{:S(2)}) async-start(), calls=%async_computation.16 | async-start | bytes 2949120 | tf_op jit(solution)/shard_map/all_gather | solution.py:205
  317.3 40.3 %copy-start.19 = (bf16[1,256,1152]{2,1,0:T(8,128)(2,1)S(1)}, bf16[1,256,1152]{2,1,0:T(8,128)(2,1)}, u32[]{:S(2)}) copy-start(bf16[1,256,1152]{2,1,0:T(8,128)(2,1)} %reduce-scatter.17.cloned.1.call-done) | copy-start | bytes 1769476
  319.7 41.1 %copy-start.15 = (bf16[1,256,1152]{2,1,0:T(8,128)(2,1)S(1)}, bf16[1,256,1152]{2,1,0:T(8,128)(2,1)}, u32[]{:S(2)}) copy-start(bf16[1,256,1152]{2,1,0:T(8,128)(2,1)} %param.29) | copy-start | bytes 1769476
  363.6 124.6 %reduce-scatter.19.cloned.1.call-start = ((), (), s32[]{:S(2)}) async-start(), calls=%async_computation.17 | async-start | bytes 2949120 | tf_op jit(solution)/shard_map/reduce_scatter | solution.py:237
  404.0 8.5 copy-start.30
  412.5 32.4 %copy-start.35 = (bf16[4,72,1024]{2,1,0:T(8,128)(2,1)}, bf16[4,72,1024]{2,1,0:T(8,128)(2,1)S(1)}, u32[]{:S(2)}) copy-start(bf16[4,72,1024]{2,1,0:T(8,128)(2,1)S(1)} %fusion.53) | copy-start | bytes 1769476
  423.5 11.8 %copy-start.26 = (bf16[1024,4,72]{0,2,1:T(8,128)(2,1)S(1)}, bf16[1024,4,72]{0,2,1:T(8,128)(2,1)}, u32[]{:S(2)}) copy-start(bf16[1024,4,72]{0,2,1:T(8,128)(2,1)} %copy-done.25) | copy-start | bytes 1769476
  450.7 38.8 %copy-start.10 = (bf16[1,256,1152]{2,1,0:T(8,128)(2,1)S(1)}, bf16[1,256,1152]{2,1,0:T(8,128)(2,1)}, u32[]{:S(2)}) copy-start(bf16[1,256,1152]{2,1,0:T(8,128)(2,1)} %param.15) | copy-start | bytes 1769476
  450.7 38.8 %copy-start.55 = (f32[256]{0:T(256)S(1)}, f32[256]{0:T(256)}, u32[]{:S(2)}) copy-start(f32[256]{0:T(256)} %copy-done.54) | copy-start | bytes 3076
  450.7 38.8 %copy-start.61 = (f32[256]{0:T(256)S(1)}, f32[256]{0:T(256)}, u32[]{:S(2)}) copy-start(f32[256]{0:T(256)} %fusion.104) | copy-start | bytes 3076
  450.8 84.2 %reduce-scatter.31.cloned.1.call-start = ((), (), s32[]{:S(2)}) async-start(), calls=%async_computation.23 | async-start | bytes 368640
  503.7 104.8 %reduce-scatter.27.cloned.1.call-start = ((), (), s32[]{:S(2)}) async-start(), calls=%async_computation.21 | async-start | bytes 7962624 | tf_op jit(solution)/shard_map/reduce_scatter | solution.py:272
  513.1 140.5 %reduce-scatter.29.cloned.1.call-start = ((), (), s32[]{:S(2)}) async-start(), calls=%async_computation.22 | async-start | bytes 3981312 | tf_op jit(solution)/shard_map/reduce_scatter | solution.py:273
  520.8 169.1 %reduce-scatter.25.cloned.1.call-start = ((), (), s32[]{:S(2)}) async-start(), calls=%async_computation.20 | async-start | bytes 1990656 | tf_op jit(solution)/shard_map/reduce_scatter | solution.py:271
  526.2 225.4 %reduce-scatter.23.cloned.1.call-start = ((), (), s32[]{:S(2)}) async-start(), calls=%async_computation.19 | async-start | bytes 5971968 | tf_op jit(solution)/shard_map/reduce_scatter | solution.py:270
  534.9 328.5 %reduce-scatter.21.cloned.1.call-start = ((), (), s32[]{:S(2)}) async-start(), calls=%async_computation.18 | async-start | bytes 11943936 | tf_op jit(solution)/shard_map/reduce_scatter | solution.py:274
  541.9 42.6 %copy-start.22 = (bf16[1,256,1152]{2,1,0:T(8,128)(2,1)S(1)}, bf16[1,256,1152]{2,1,0:T(8,128)(2,1)}, u32[]{:S(2)}) copy-start(bf16[1,256,1152]{2,1,0:T(8,128)(2,1)} %reduce-scatter.19.cloned.1.call-done) | copy-start | bytes 1769476
  588.2 275.2 %copy-start.1 = (bf16[1152,2,768]{2,1,0:T(2,128)(2,1)S(1)}, bf16[1152,2,768]{2,1,0:T(2,128)(2,1)}, u32[]{:S(2)}) copy-start(bf16[1152,2,768]{2,1,0:T(2,128)(2,1)} %param.23) | copy-start | bytes 10616836
  (69 other events, 156.9 us)
Sparse Core Ops, SparseCore 0:
  49.0 37.7 all-gather.4
  124.3 57.0 reduce-scatter.12
  188.4 37.4 all-gather.6
  228.2 37.4 all-gather.8
  279.9 37.3 reduce-scatter.16
  320.2 37.3 reduce-scatter.14
  363.8 37.4 all-gather.10
  450.8 37.3 reduce-scatter.18
  503.8 24.1 reduce-scatter.30
  530.2 78.2 reduce-scatter.26
  611.4 42.1 reduce-scatter.28
  656.5 33.3 reduce-scatter.24
  692.9 58.6 reduce-scatter.22
  754.4 108.9 reduce-scatter.20
where the time goes:
time: 876 us; the launch traced here: 870 us
  waiting for transfers between devices  574 us (66%)
  matrix products  126 us (14%)
  other arithmetic  59.1 us (7%)
  blocking collectives  59.1 us (7%)
  local copies, waits for them, and re-layouts  35.6 us (4%)
  between operations  15.4 us (2%)
    reduce_scatter x1, waiting for transfers between devices, shards(): lax.psum_scatter(modulator_grad, 'dp', scatter_dimension=0, tiled=True)  112 us
    reduce_scatter x1, waiting for transfers between devices, shards(): lax.psum_scatter(inward_grad, 'dp', scatter_dimension=0, tiled=True)  61.7 us
    reduce_scatter x1, waiting for transfers between devices, shards(): lax.psum_scatter(jnp.einsum('sli,oi->slo', mixed_low, outward, preferred_...  57.2 us
    reduce_scatter x1, waiting for transfers between devices, shards(): lax.psum_scatter(contraction_grad, 'dp', scatter_dimension=0, tiled=True)  42.4 us
    psum x1, blocking collectives, shards(): lax.psum((query_scale_grad, key_scale_grad, jnp.sum(slot_grad, axis=0)),...  42 us
    reduce_scatter x1, waiting for transfers between devices, shards(): lax.psum_scatter(jnp.einsum('slf,of->slo', hidden, contraction, preferred...  37.9 us
    all_gather x1, waiting for transfers between devices, shards(): lax.all_gather((gate_one * middle_grad).astype(jnp.bfloat16), 'tp', axis=...  37.4 us
    reduce_scatter x1, waiting for transfers between devices, shards(): lax.psum_scatter(jnp.einsum('tqkf,ckf->tqc', projected_rows_gradient, inw...  37.3 us
  transfers between devices with their start and end apart: 14, of which 13 were waited for; matrix products, arithmetic and copies ran while one was open for 7% of the time, Pallas kernels for 0%

commit v1 on v0

v1 whole, which is shorter than its diff:
```python
import math

import jax
import jax.numpy as jnp
from jax import lax
from jax.sharding import PartitionSpec as P

BF = jnp.bfloat16
F32 = jnp.float32


def dot(left, right, dims):
    return lax.dot_general(left, right, (dims, ((), ())), preferred_element_type=F32)


def flip(value, by):
    return lax.ppermute(value, "tp", [(i, i ^ by) for i in range(4)])


def gather_tp(own):
    half = own.shape[0] // 2
    one, two = flip(own, 1), flip(own, 2)
    three = (flip(one[:half], 2), flip(two[half:], 1))
    return [own, one, two, jnp.concatenate(three, axis=0)]


def scatter_tp(parts):
    half = parts[0].shape[0] // 2
    low = [part.astype(BF) for part in parts[1:]]
    via_one, via_two = flip(low[2][:half], 1), flip(low[2][half:], 2)
    for_one = jnp.concatenate([low[0][:half], low[0][half:] + via_two], axis=0)
    for_two = jnp.concatenate([low[1][:half] + via_one, low[1][half:]], axis=0)
    return parts[0].astype(F32) + flip(for_one, 1).astype(F32) + flip(for_two, 2).astype(F32)


def gather_small(own, dp):
    if dp != 8:
        return lax.all_gather(own, "dp", axis=0)
    me = lax.axis_index("dp")

    def swap(value, by):
        return lax.ppermute(value, "dp", [(i, i ^ by) for i in range(dp)])

    other = swap(own, 1)
    core = me % 2
    pair = jnp.where(core == 0, jnp.stack([own, other]), jnp.stack([other, own]))
    pairs = jnp.stack([pair, swap(pair, 2), swap(pair, 4), swap(pair, 6)])
    place = me // 2
    ordered = jnp.take(pairs, jnp.arange(4) ^ place, axis=0)
    return ordered.reshape((dp,) + own.shape)


def sum_tp_columns(values):
    cut = values.shape[-1] // 4
    me = lax.axis_index("tp")

    def piece(k):
        return lax.dynamic_slice_in_dim(values, (me ^ k) * cut, cut, values.ndim - 1)

    return piece(0) + flip(piece(1), 1) + flip(piece(2), 2) + flip(piece(3), 3)


def gather_tp_columns(own):
    me = lax.axis_index("tp")
    rel = jnp.stack([own, flip(own, 1), flip(own, 2), flip(own, 3)])
    ordered = jnp.take(rel, jnp.arange(4) ^ me, axis=0)
    return jnp.moveaxis(ordered, 0, -2).reshape(own.shape[:-1] + (4 * own.shape[-1],))


def norm(values):
    center = values - jnp.mean(values, axis=-1, keepdims=True)
    inverse = lax.rsqrt(jnp.mean(center * center, axis=-1, keepdims=True) + 1e-06)
    return center * inverse, inverse


def norm_back(grad, normed, inverse):
    return inverse * (
        grad
        - jnp.mean(grad, axis=-1, keepdims=True)
        - normed * jnp.mean(grad * normed, axis=-1, keepdims=True)
    )


def turn_half(values):
    quarter = values.shape[-1] // 4
    a, b, c, d = [values[..., i * quarter : (i + 1) * quarter] for i in range(4)]
    return jnp.concatenate([-b, a, -d, c], axis=-1)


def prepare(raw, gain, cosine, sine):
    normed = raw * lax.rsqrt(jnp.mean(raw * raw, axis=-1, keepdims=True) + 1e-06) * gain
    return normed * cosine + turn_half(normed) * sine


def masked_scores(queries, keys, owners):
    factor = 1.0 / math.sqrt(queries.shape[-1])
    scores = jnp.einsum("qhe,khe->hqk", queries, keys, preferred_element_type=F32) * factor
    return jnp.where((owners[:, None] == owners[None, :])[None], scores, -1e30)


def shards(
    tokens,
    condition,
    modulator,
    offsets,
    inward,
    query_gain,
    key_gain,
    outward,
    expansion,
    contraction,
    item_lengths,
    item_condition,
    patch_rows,
    patch_columns,
    cotangent,
):
    _, rows, width = tokens.shape
    full = patch_rows.shape[1]
    head = query_gain.shape[0]
    heads = inward.shape[2] // head
    part = inward.shape[2]
    dp = lax.axis_size("dp")
    me = lax.axis_index("tp")
    dp_me = lax.axis_index("dp")
    lanes = width // dp

    x = tokens[0]
    x_all = gather_tp(x)
    cond_low = jax.nn.silu(condition.astype(F32)).astype(BF)
    share = dot(cond_low, modulator, ((1,), (0,)))
    table = gather_tp_columns(share) + offsets
    dy = cotangent[0]
    dy_all = gather_tp(dy)
    cond_all = gather_small(cond_low, dp).reshape(2 * dp, width)

    order = jnp.arange(4) ^ me

    def relative(values):
        return jnp.take(values.reshape(4, rows), order, axis=0).reshape(full)

    ends = jnp.cumsum(item_lengths[0])
    owners = jnp.sum((jnp.arange(full)[:, None] >= ends[None, :]).astype(jnp.int32), axis=-1)
    owners = relative(owners)
    item_hot = owners[:, None] == jnp.arange(item_lengths.shape[1])
    second = jnp.sum(jnp.where(item_hot, item_condition[0][None, :], 0), axis=-1) == 1
    second = second[:, None]

    def per_token(column, k):
        pick = second[k * rows : (k + 1) * rows]
        return jnp.where(pick, table[1, column], table[0, column])

    quarter = head // 4
    frequency = 10000.0 ** (-jnp.arange(quarter, dtype=F32) / quarter)
    along_rows = relative(patch_rows[0]).astype(F32)[:, None] * frequency
    along_columns = relative(patch_columns[0]).astype(F32)[:, None] * frequency
    angles = jnp.concatenate([along_rows, along_rows, along_columns, along_columns], axis=-1)
    cosine, sine = jnp.cos(angles)[:, None], jnp.sin(angles)[:, None]

    inward_flat = inward.reshape(width, 3 * part)
    expansion_flat = expansion.reshape(width, -1)
    first_in, first_normed, first_inverse, projected = [], [], [], []
    for k in range(4):
        normed, inverse = norm(x_all[k].astype(F32))
        low = (normed * (1.0 + per_token(1, k)) + per_token(0, k)).astype(BF)
        first_in.append(low)
        if k == 0:
            first_normed, first_inverse = normed, inverse
        projected.append(dot(low, inward_flat, ((1,), (0,))))
    first_in = jnp.concatenate(first_in, axis=0)
    projected = jnp.concatenate(projected, axis=0).reshape(full, 3, heads, head)
    query_raw, key_raw = projected[:, 0], projected[:, 1]
    queries = prepare(query_raw, query_gain, cosine, sine).astype(BF)
    keys = prepare(key_raw, key_gain, cosine, sine).astype(BF)
    values = projected[:, 2].astype(BF)

    scores = masked_scores(queries, keys, owners)
    top = jnp.max(scores, axis=-1, keepdims=True)
    weights = jnp.exp(scores - top)
    total = jnp.sum(weights, axis=-1, keepdims=True)
    rounded = (weights / total).astype(BF)
    mixed = jnp.einsum("hqk,khe->qhe", rounded, values, preferred_element_type=F32)
    log_total = top + jnp.log(total)
    mixed_low = mixed.reshape(full, part).astype(BF)

    def cut(array, k):
        return array[k * rows : (k + 1) * rows]

    attended = scatter_tp([dot(cut(mixed_low, k), outward, ((1,), (1,))) for k in (0, 1, 2, 3)])
    stream = x.astype(F32)
    gate_one = per_token(2, 0)
    middle = stream + gate_one * attended
    second_normed, second_inverse = norm(middle)
    second_scale = 1.0 + per_token(4, 0)
    second_own = (second_normed * second_scale + per_token(3, 0)).astype(BF)
    second_all = gather_tp(second_own)
    fed_grad = jnp.concatenate(
        [(per_token(5, k) * dy_all[k].astype(F32)).astype(BF) for k in range(4)], axis=0
    )
    hidden_grad = dot(fed_grad, contraction, ((1,), (0,)))
    hidden, widening, second_parts, fed_parts = [], [], [], []
    units = contraction.shape[1]
    for k in range(4):
        both = dot(second_all[k], expansion_flat, ((1,), (0,)))
        gate, up = both[:, :units], both[:, units:]
        sigmoid = jax.nn.sigmoid(gate)
        active = gate * sigmoid
        hidden.append((active * up).astype(BF))
        grad = cut(hidden_grad, k)
        gate_grad = grad * up * (sigmoid + active * (1.0 - sigmoid))
        widening.append(jnp.concatenate([gate_grad, grad * active], axis=1).astype(BF))
        second_parts.append(dot(widening[k], expansion_flat, ((1,), (1,))))
    second_grad = scatter_tp(second_parts)
    fed_parts = [dot(hidden[k], contraction, ((1,), (1,))) for k in range(4)]
    fed = scatter_tp(fed_parts)
    upstream = dy.astype(F32)
    layer_output = (middle + per_token(5, 0) * fed).astype(BF)
    hidden = jnp.concatenate(hidden, axis=0)
    widening = jnp.concatenate(widening, axis=0)
    second_in = jnp.concatenate(second_all, axis=0)
    wide = jnp.concatenate(
        [
            dot(second_in, widening, ((0,), (0,))).astype(BF),
            dot(fed_grad, hidden, ((0,), (0,))).astype(BF),
        ],
        axis=1,
    )
    wide = lax.psum_scatter(wide, "dp", scatter_dimension=0, tiled=True)

    middle_grad = upstream + norm_back(second_grad * second_scale, second_normed, second_inverse)
    attended_grad = jnp.concatenate(gather_tp((gate_one * middle_grad).astype(BF)), axis=0)
    mixed_grad = dot(attended_grad, outward, ((1,), (0,))).astype(BF)
    outward_grad = dot(attended_grad, mixed_low, ((0,), (0,)))
    mixed_grad = mixed_grad.reshape(full, heads, head)

    factor = 1.0 / math.sqrt(head)
    weights = jnp.exp(masked_scores(queries, keys, owners) - log_total)
    value_grad = jnp.einsum("hqk,qhe->khe", weights.astype(BF), mixed_grad, preferred_element_type=F32)
    weight_grad = jnp.einsum("qhe,khe->hqk", mixed_grad, values, preferred_element_type=F32)
    centre = jnp.sum(weights * weight_grad, axis=-1, keepdims=True)
    score_grad = (weights * (weight_grad - centre)).astype(BF)
    query_grad = jnp.einsum("hqk,khe->qhe", score_grad, keys, preferred_element_type=F32) * factor
    key_grad = jnp.einsum("hqk,qhe->khe", score_grad, queries, preferred_element_type=F32) * factor

    def both_heads(query_in, key_in, query_scale, key_scale):
        return (
            prepare(query_in, query_scale, cosine, sine),
            prepare(key_in, key_scale, cosine, sine),
        )

    _, pull = jax.vjp(both_heads, query_raw, key_raw, query_gain, key_gain)
    query_raw_grad, key_raw_grad, query_gain_grad, key_gain_grad = pull((query_grad, key_grad))
    projected_grad = jnp.stack([query_raw_grad, key_raw_grad, value_grad], axis=1)
    projected_grad = projected_grad.reshape(full, 3 * part).astype(BF)
    inward_grad = dot(first_in, projected_grad, ((0,), (0,)))
    narrow = jnp.concatenate([inward_grad.astype(BF), outward_grad.astype(BF)], axis=1)
    narrow = lax.psum_scatter(narrow, "dp", scatter_dimension=0, tiled=True)
    first_grad = scatter_tp([dot(cut(projected_grad, k), inward_flat, ((1,), (1,))) for k in range(4)])
    token_gradient = middle_grad + norm_back(
        first_grad * (1.0 + per_token(1, 0)), first_normed, first_inverse
    )

    pick = second[:rows]

    def slots(values):
        return jnp.stack([jnp.sum(jnp.where(pick, 0.0, values), axis=0), jnp.sum(jnp.where(pick, values, 0.0), axis=0)])

    mod = jnp.stack(
        [
            slots(first_grad),
            slots(first_grad * first_normed),
            slots(middle_grad * attended),
            slots(second_grad),
            slots(second_grad * second_normed),
            slots(upstream * fed),
        ],
        axis=1,
    )
    gains = jnp.concatenate([query_gain_grad, key_gain_grad])
    gains = jnp.pad(gains, (0, part - 2 * head))
    gains = jnp.broadcast_to(gains, (1, 4, part)).reshape(1, 4 * part)
    flat = jnp.concatenate([mod.reshape(12, width), gains], axis=0)
    every = gather_small(sum_tp_columns(flat), dp)
    gain_sum = jnp.sum(every[:, 12], axis=0)
    slot_share = every[:, :12].reshape(2 * dp, 6, part)
    bias_gradient = gather_tp_columns(jnp.sum(slot_share, axis=0))
    cond_rows = lax.dynamic_slice_in_dim(cond_all, dp_me * lanes, lanes, 1).astype(F32)
    modulator_gradient = jnp.einsum("cd,cje->dje", cond_rows, slot_share, precision=lax.Precision.HIGHEST)

    wide, narrow = wide.astype(F32), narrow.astype(F32)
    return (
        layer_output[None],
        token_gradient[None],
        modulator_gradient,
        bias_gradient,
        narrow[:, : 3 * part].reshape(lanes, 3, part),
        gain_sum[:head],
        gain_sum[head : 2 * head],
        narrow[:, 3 * part :],
        wide[:, : 2 * units].reshape(lanes, 2, units),
        wide[:, 2 * units :],
    )


def solution(mesh):
    placed = (
        P("dp", "tp", None),
        P("dp", None),
        P(None, None, "tp"),
        P(),
        P(None, None, "tp"),
        P(),
        P(),
        P(None, "tp"),
        P(None, None, "tp"),
        P(None, "tp"),
        P("dp", None),
        P("dp", None),
        P("dp", None),
        P("dp", None),
        P("dp", "tp", None),
    )
    return jax.shard_map(
        shards,
        mesh=mesh,
        in_specs=placed,
        out_specs=(
            P("dp", "tp", None),
            P("dp", "tp", None),
            P("dp", None, "tp"),
            P(),
            P("dp", None, "tp"),
            P(),
            P(),
            P("dp", "tp"),
            P("dp", None, "tp"),
            P("dp", "tp"),
        ),
        check_vma=False,
    )
```

time: 876 us -> 412 us (0.47)
  waiting for transfers between devices: 574 us -> 129 us
  starting transfers between devices: 1.43 us -> 60.6 us
  blocking collectives: 59.1 us -> 0 us
  matrix products: 126 us -> 95 us
    reduce_scatter x9 -> x1, waiting for transfers between devices: 433 us -> 31 us  [shards(): wide = lax.psum_scatter(wide, 'dp', scatter_dimension=0, tiled=True)]
    all_gather x4 -> x0, waiting for transfers between devices: 140 us -> none  [the longest x1 37.4 us: shards(): lax.all_gather((gate_one * middle_grad).astype(jnp.bfloat16), 'tp', axis=...]
    ppermute x0 -> x49, waiting for transfers between devices: none -> 97.7 us  [the longest x41 86.8 us: flip(): return lax.ppermute(value, 'tp', [(i, i ^ by) for i in range(4)])]
    ppermute x0 -> x49, starting transfers between devices: none -> 60.5 us  [the longest x41 51.5 us: flip(): return lax.ppermute(value, 'tp', [(i, i ^ by) for i in range(4)])]
    psum x1 -> x0, blocking collectives: 42 us -> none  [shards(): lax.psum((query_scale_grad, key_scale_grad, jnp.sum(slot_grad, axis=0)),...]
    dot_general x22 -> x38, matrix products: 126 us -> 95 us  [the longest x31 53.8 us: dot(): lax.dot_general(left, right, (dims, ((), ())), preferred_element_type=F32)]
    all_gather x1 -> x0, blocking collectives: 17.1 us -> none  [shards(): lax.all_gather(local_shares, 'tp', axis=2, tiled=True) + offsets]
    slice x2 -> x21, local copies, waits for them, and re-layouts: 0.24 us -> 9.18 us  [the longest x8 3.09 us: gather_tp(): three = (flip(one[:half], 2), flip(two[half:], 1))]
  transfers between devices with their start and end apart: 14 -> 51, of which waited for: 13 -> 27; matrix products, arithmetic and copies ran while one was open for 7% -> 28% of each run, Pallas kernels for 0% -> 0%
where the time goes in v1:
time: 412 us; the launch traced here: 409 us
  waiting for transfers between devices  129 us (31%)
  matrix products  95 us (23%)
  other arithmetic  66.3 us (16%)
  starting transfers between devices  60.6 us (15%)
  local copies, waits for them, and re-layouts  41.4 us (10%)
  between operations  16.8 us (4%)
    ppermute x41, waiting for transfers between devices, flip(): return lax.ppermute(value, 'tp', [(i, i ^ by) for i in range(4)])  86.8 us
    dot_general x31, matrix products, dot(): lax.dot_general(left, right, (dims, ((), ())), preferred_element_type=F32)  53.8 us
    ppermute x41, starting transfers between devices, flip(): return lax.ppermute(value, 'tp', [(i, i ^ by) for i in range(4)])  51.5 us
    reduce_scatter x1, waiting for transfers between devices, shards(): wide = lax.psum_scatter(wide, 'dp', scatter_dimension=0, tiled=True)  31 us
    unnamed x278, local copies, waits for them, and re-layouts  22.8 us
    dot_general x1, matrix products, shards(): jnp.einsum('qhe,khe->hqk', mixed_grad, values, preferred_element_type=F32)  15 us
    convert_element_type x1, other arithmetic, shards(): score_grad = (weights * (weight_grad - centre)).astype(BF)  12.2 us
    ppermute x8, waiting for transfers between devices, swap(): return lax.ppermute(value, 'dp', [(i, i ^ by) for i in range(dp)])  10.9 us
  transfers between devices with their start and end apart: 51, of which 27 were waited for; matrix products, arithmetic and copies ran while one was open for 28% of the time, Pallas kernels for 0%

profile of v1, /device:TPU:0, one launch (start us, length us, event | category | flops | bytes accessed | tf_op | source)
XLA Modules:
  0.0 408.8 jit_solution(4029562978706572567)
XLA Ops:
  7.3 3.6 fusion.144
  10.9 4.0 collective-permute-start.2
  44.4 5.9 %collective-permute-done.5 = bf16[128,1152]{1,0:T(8,128)(2,1)S(1)} collective-permute-done((bf16[128,1152]{1,0:T(8,128)(2,1)S(1)}, bf16[128,1152]{1,0:T(8,128)(2,1)S(1)}, u32[]{:S(2)}, u32[]{:S(2)}) %collective-permute-start.5) | collective-permute-done | bytes 294944 | tf_op jit(solution)/shard_map/ppermute | solution.py:17
  60.7 7.5 %fusion.177 = (f32[4,1024]{1,0:T(4,128)S(1)}, f32[4,1024,1024]{1,2,0:T(8,128)}) fusion(bf16[1024,4,72]{0,2,1:T(8,128)(2,1)S(1)} %get-tuple-element.186, bf16[1024,4,72]{0,2,1:T(8,128)(2,1)S(1)} %get-tuple-element.185, pred[1024,1024]{0,1:T(8,128)(4,1)S(1)} %copy-done.8), kind=kOutput, calls=%fused_computation.406 | convolution fusion | flops 616558592 | bytes 19021824 | tf_op jit(solution)/shard_map/qhe,khe->hqk/dot_general | solution.py:97
  68.2 8.0 %fusion = f32[4,1024]{1,0:T(4,128)S(1)} fusion(f32[4,1024,1024]{1,2,0:T(8,128)} %get-tuple-element.217, f32[4,1024]{1,0:T(4,128)S(1)} %get-tuple-element.216), kind=kLoop, calls=%fused_computation.13 | loop fusion | flops 8384512 | bytes 16809984 | tf_op jit(solution)/shard_map/reduce_sum | solution.py:180
  76.2 7.8 %fusion.50 = bf16[4,72,1024]{2,1,0:T(8,128)(2,1)S(1)} fusion(f32[4,1024,1024]{1,2,0:T(8,128)} %get-tuple-element.217, f32[4,1024]{1,0:T(4,128)S(1)} %fusion, f32[4,1024]{1,0:T(4,128)S(1)} %get-tuple-element.216, f32[1024,3,4,72]{0,3,2,1:T(8,128)S(1)} %bitcast.213), kind=kOutput, calls=%fused_computation.102 | convolution fusion | flops 616857600 | bytes 17989632 | tf_op jit(solution)/shard_map/hqk,khe->qhe/dot_general | solution.py:182
  89.1 3.6 collective-permute-done.9
  102.3 11.0 %collective-permute-done.21 = bf16[128,1152]{1,0:T(8,128)(2,1)S(1)} collective-permute-done((bf16[128,1152]{1,0:T(8,128)(2,1)S(1)}, bf16[128,1152]{1,0:T(8,128)(2,1)S(1)}, u32[]{:S(2)}, u32[]{:S(2)}) %collective-permute-start.21) | collective-permute-done | bytes 294944 | tf_op jit(solution)/shard_map/ppermute | solution.py:17
  114.5 3.9 fusion.77
  126.3 6.0 %collective-permute-done.13 = bf16[256,1152]{1,0:T(8,128)(2,1)S(1)} collective-permute-done((bf16[256,1152]{1,0:T(8,128)(2,1)S(1)}, bf16[256,1152]{1,0:T(8,128)(2,1)S(1)}, u32[]{:S(2)}, u32[]{:S(2)}) %collective-permute-start.13) | collective-permute-done | bytes 589856 | tf_op jit(solution)/shard_map/ppermute | solution.py:17
  153.8 5.9 %collective-permute-done.17 = bf16[128,1152]{1,0:T(8,128)(2,1)S(1)} collective-permute-done((bf16[128,1152]{1,0:T(8,128)(2,1)S(1)}, bf16[128,1152]{1,0:T(8,128)(2,1)S(1)}, u32[]{:S(2)}, u32[]{:S(2)}) %collective-permute-start.17) | collective-permute-done | bytes 294944 | tf_op jit(solution)/shard_map/ppermute | solution.py:17
  159.8 3.0 collective-permute-start.18
  167.6 9.5 %collective-permute-done.18 = bf16[256,1152]{1,0:T(8,128)(2,1)S(1)} collective-permute-done((bf16[256,1152]{1,0:T(8,128)(2,1)S(1)}, bf16[256,1152]{1,0:T(8,128)(2,1)S(1)}, u32[]{:S(2)}, u32[]{:S(2)}) %collective-permute-start.18) | collective-permute-done | bytes 589856 | tf_op jit(solution)/shard_map/ppermute | solution.py:17
  178.7 6.2 %collective-permute-done.26 = bf16[256,1152]{1,0:T(8,128)(2,1)S(1)} collective-permute-done((bf16[256,1152]{1,0:T(8,128)(2,1)S(1)}, bf16[256,1152]{1,0:T(8,128)(2,1)S(1)}, u32[]{:S(2)}, u32[]{:S(2)}) %collective-permute-start.26) | collective-permute-done | bytes 589856 | tf_op jit(solution)/shard_map/ppermute | solution.py:17
  185.0 2.8 select_reduce_fusion.3
  187.8 2.9 constant_dynamic-update-slice_fusion.4
  193.5 9.8 %collective-permute-done.28 = bf16[256,1152]{1,0:T(8,128)(2,1)S(1)} collective-permute-done((bf16[256,1152]{1,0:T(8,128)(2,1)S(1)}, bf16[256,1152]{1,0:T(8,128)(2,1)S(1)}, u32[]{:S(2)}, u32[]{:S(2)}) %collective-permute-start.28) | collective-permute-done | bytes 589856 | tf_op jit(solution)/shard_map/ppermute | solution.py:17
  206.4 5.8 %collective-permute-done.29 = bf16[128,1152]{1,0:T(8,128)(2,1)S(1)} collective-permute-done((bf16[128,1152]{1,0:T(8,128)(2,1)S(1)}, bf16[128,1152]{1,0:T(8,128)(2,1)S(1)}, u32[]{:S(2)}, u32[]{:S(2)}) %collective-permute-start.29) | collective-permute-done | bytes 294944 | tf_op jit(solution)/shard_map/ppermute | solution.py:17
  214.1 4.6 %fusion.51 = bf16[1024,1,4,72]{0,3,2,1:T(8,128)(2,1)} fusion(bf16[1024,4,72]{0,2,1:T(8,128)(2,1)} %bitcast.230, f32[4,1024,1024]{1,2,0:T(8,128)S(1)} %bitcast.210, f32[4,1024]{1,0:T(4,128)S(1)} %log_add_fusion), kind=kOutput, calls=%fused_computation.103 | convolution fusion | flops 612663296 | bytes 17973248 | tf_op jit(solution)/shard_map/hqk,qhe->khe/dot_general | solution.py:238
  218.7 15.0 %multiply_reduce_fusion = (f32[4,1024]{1,0:T(4,128)S(1)}, f32[4,1024,1024]{1,2,0:T(8,128)}) fusion(f32[4,1024,1024]{1,2,0:T(8,128)} %get-tuple-element.217, f32[4,1024]{1,0:T(4,128)S(1)} %log_add_fusion, bf16[1024,4,72]{0,2,1:T(8,128)(2,1)} %bitcast.231, f32[1024,3,4,72]{0,3,2,1:T(8,128)} %bitcast.214), kind=kOutput, calls=%fused_computation.8 | convolution fusion | flops 616558592 | bytes 34766848 | tf_op jit(solution)/shard_map/qhe,khe->hqk/dot_general | solution.py:239
  233.7 12.2 %multiply_convert_fusion = bf16[4,1024,1024]{1,2,0:T(8,128)(2,1)S(1)} fusion(f32[4,1024,1024]{1,2,0:T(8,128)} %get-tuple-element.220, f32[4,1024,1024]{1,2,0:T(8,128)} %get-tuple-element.217, f32[4,1024]{1,0:T(4,128)S(1)} %get-tuple-element.219, f32[4,1024]{1,0:T(4,128)S(1)} %log_add_fusion), kind=kLoop, calls=%fused_computation.7 | loop fusion | flops 16777216 | bytes 41975808 | tf_op jit(solution)/shard_map/convert_element_type | solution.py:241
  260.9 8.1 %collective-permute-done.33 = bf16[128,1152]{1,0:T(8,128)(2,1)S(1)} collective-permute-done((bf16[128,1152]{1,0:T(8,128)(2,1)S(1)}, bf16[128,1152]{1,0:T(8,128)(2,1)S(1)}, u32[]{:S(2)}, u32[]{:S(2)}) %collective-permute-start.33) | collective-permute-done | bytes 294944 | tf_op jit(solution)/shard_map/ppermute | solution.py:17
  273.6 5.4 %collective-permute-done.34 = bf16[256,1152]{1,0:T(8,128)(2,1)S(1)} collective-permute-done((bf16[256,1152]{1,0:T(8,128)(2,1)S(1)}, bf16[256,1152]{1,0:T(8,128)(2,1)S(1)}, u32[]{:S(2)}, u32[]{:S(2)}) %collective-permute-start.34) | collective-permute-done | bytes 589856 | tf_op jit(solution)/shard_map/ppermute | solution.py:17
  280.6 4.6 %select_reduce_fusion.1 = (f32[1152]{0:T(1024)S(1)}, f32[1152]{0:T(1024)S(1)}, f32[1152]{0:T(1024)S(1)}, f32[1152]{0:T(1024)S(1)}, f32[256]{0:T(256)}, /*index=5...) fusion(pred[256]{0:T(512)(128)(4,1)S(1)} %copy-done.97, ...), kind=kLoop, calls=%fused_computation.142 | loop fusion | flops 13261312 | bytes 11266304 | tf_op jit(solution)/shard_map/reduce_sum | solution.py:266
  289.3 5.2 %copy.97 = bf16[1152,1152]{1,0:T(8,128)(2,1)} copy(bf16[1152,1152]{0,1:T(8,128)(2,1)} %pad_maximum_fusion.2) | data formatting | bytes 5308416
  300.1 3.5 convolution_convert_fusion.2
  303.7 14.8 %convolution_convert_fusion = bf16[1152,1536]{1,0:T(8,128)(2,1)S(1)} fusion(bf16[1024,1152]{1,0:T(8,128)(2,1)S(1)} %copy-done.76, bf16[256,768]{1,0:T(8,128)(2,1)S(1)} %copy-done.55, bf16[256,768]{1,0:T(8,128)(2,1)S(1)} %copy-done.57, bf16[256,768]{1,0:T(8,128)(2,1)S(1)} %copy-done.66, bf16[256,768]{1,0:T(8,128)(2,1)S(1)} %copy-done.64, ...), kind=kOutput, calls=%fused_computation.18 | convolution fusion | flops 3650813952 | bytes 9043968 | tf_op jit(solution)/shard_map/dot_general | solution.py:13
  323.2 3.3 collective-permute-start.38
  339.4 3.3 fusion.58
  347.2 3.0 collective-permute-done.45
  350.2 3.7 collective-permute-done.44
  366.5 31.0 %reduce-scatter.5.cloned.1.call-done = bf16[144,2304]{1,0:T(8,128)(2,1)} async-done(((bf16[1152,2304]{1,0:T(8,128)(2,1)}), bf16[144,2304]{1,0:T(8,128)(2,1)}) %reduce-scatter.5.cloned.1.call-update) | async-done | bytes 663568 | tf_op jit(solution)/shard_map/reduce_scatter | solution.py:228
  (567 shorter events, 167.3 us)
Async XLA Ops:
  7.2 355.7 %reduce-scatter.7.cloned.1.call-start = ((), (), s32[]{:S(2)}) async-start(), calls=%async_computation.3 | async-start | bytes 2985984
  10.9 18.6 %collective-permute-start.2 = (f32[2,6,288]{2,0,1:T(2,128)S(1)}, f32[2,6,288]{2,0,1:T(2,128)S(1)}, u32[]{:S(2)}, u32[]{:S(2)}) collective-permute-start(f32[2,6,288]{2,0,1:T(2,128)S(1)} %fusion.144), channel_id=1, source_target_pairs={{0,24},{8,16},{16,8},{24,0},{1,25},{9,17},{17,9},{25,1},{2,26},{10... | collective-permute-start | bytes 41480 | tf_op jit(solution)/shard_map/ppermute | solution.py:17
  14.9 15.1 %collective-permute-start.1 = (f32[2,6,288]{2,0,1:T(2,128)S(1)}, f32[2,6,288]{2,0,1:T(2,128)S(1)}, u32[]{:S(2)}, u32[]{:S(2)}) collective-permute-start(f32[2,6,288]{2,0,1:T(2,128)S(1)} %fusion.144), channel_id=1, source_target_pairs={{0,16},{8,24},{16,0},{24,8},{1,17},{9,25},{17,1},{25,9},{2,18},{10... | collective-permute-start | bytes 41480 | tf_op jit(solution)/shard_map/ppermute | solution.py:17
  15.4 14.7 %collective-permute-start = (f32[2,6,288]{2,0,1:T(2,128)S(1)}, f32[2,6,288]{2,0,1:T(2,128)}, u32[]{:S(2)}, u32[]{:S(2)}) collective-permute-start(f32[2,6,288]{2,0,1:T(2,128)S(1)} %fusion.144), channel_id=1, source_target_pairs={{0,8},{8,0},{16,24},{24,16},{1,9},{9,1},{17,25},{25,17},{2,10},{10... | collective-permute-start | bytes 41480 | tf_op jit(solution)/shard_map/ppermute | solution.py:17
  15.5 21.6 %collective-permute-start.3 = (bf16[256,1152]{1,0:T(8,128)(2,1)S(1)}, bf16[256,1152]{1,0:T(8,128)(2,1)S(1)}, u32[]{:S(2)}, u32[]{:S(2)}) collective-permute-start(bf16[256,1152]{1,0:T(8,128)(2,1)S(1)} %bitcast.217), channel_id=1, source_target_pairs={{0,8},{8,0},{16,24},{24,16},{1,9},{9,1},{17,25},{25,17},{2,10},{10... | collective-permute-start | bytes 1769480 | tf_op jit(solution)/shard_map/ppermute | solution.py:17
  17.4 21.8 %collective-permute-start.4 = (bf16[256,1152]{1,0:T(8,128)(2,1)S(1)}, bf16[256,1152]{1,0:T(8,128)(2,1)}, u32[]{:S(2)}, u32[]{:S(2)}) collective-permute-start(bf16[256,1152]{1,0:T(8,128)(2,1)S(1)} %bitcast.218), channel_id=1, source_target_pairs={{0,16},{8,24},{16,0},{24,8},{1,17},{9,25},{17,1},{25,9},{2,18},{10... | collective-permute-start | bytes 1769480 | tf_op jit(solution)/shard_map/ppermute | solution.py:17
  29.5 68.1 %collective-permute-start.19 = (bf16[256,1152]{1,0:T(8,128)(2,1)}, bf16[256,1152]{1,0:T(8,128)(2,1)}, u32[]{:S(2)}, u32[]{:S(2)}) collective-permute-start(bf16[256,1152]{1,0:T(8,128)(2,1)} %bitcast.23), channel_id=1, source_target_pairs={{0,8},{8,0},{16,24},{24,16},{1,9},{9,1},{17,25},{25,17},{2,10},{10... | collective-permute-start | bytes 1769480 | tf_op jit(solution)/shard_map/ppermute | solution.py:17
  30.0 70.4 %collective-permute-start.20 = (bf16[256,1152]{1,0:T(8,128)(2,1)}, bf16[256,1152]{1,0:T(8,128)(2,1)}, u32[]{:S(2)}, u32[]{:S(2)}) collective-permute-start(bf16[256,1152]{1,0:T(8,128)(2,1)} %bitcast.23), channel_id=1, source_target_pairs={{0,16},{8,24},{16,0},{24,8},{1,17},{9,25},{17,1},{25,9},{2,18},{10... | collective-permute-start | bytes 1769480 | tf_op jit(solution)/shard_map/ppermute | solution.py:17
  37.2 13.1 %collective-permute-start.5 = (bf16[128,1152]{1,0:T(8,128)(2,1)S(1)}, bf16[128,1152]{1,0:T(8,128)(2,1)S(1)}, u32[]{:S(2)}, u32[]{:S(2)}) collective-permute-start(bf16[128,1152]{1,0:T(8,128)(2,1)S(1)} %slice.441), channel_id=1, source_target_pairs={{0,16},{8,24},{16,0},{24,8},{1,17},{9,25},{17,1},{25,9},{2,18},{10... | collective-permute-start | bytes 884744 | tf_op jit(solution)/shard_map/ppermute | solution.py:17
  92.8 21.6 %collective-permute-start.10 = (bf16[256,1152]{1,0:T(8,128)(2,1)S(1)}, bf16[256,1152]{1,0:T(8,128)(2,1)S(1)}, u32[]{:S(2)}, u32[]{:S(2)}) collective-permute-start(bf16[256,1152]{1,0:T(8,128)(2,1)S(1)} %pad_maximum_fusion.7), channel_id=1, source_target_pairs={{0,16},{8,24},{16,0},{24,8},{1,17},{9,25},{17,1},{25,9},{2,18},{10... | collective-permute-start | bytes 1769480 | tf_op jit(solution)/shard_map/ppermute | solution.py:17
  95.4 19.1 %collective-permute-start.8 = (bf16[256,1152]{1,0:T(8,128)(2,1)S(1)}, bf16[256,1152]{1,0:T(8,128)(2,1)S(1)}, u32[]{:S(2)}, u32[]{:S(2)}) collective-permute-start(bf16[256,1152]{1,0:T(8,128)(2,1)S(1)} %pad_maximum_fusion.6), channel_id=1, source_target_pairs={{0,8},{8,0},{16,24},{24,16},{1,9},{9,1},{17,25},{25,17},{2,10},{10... | collective-permute-start | bytes 1769480 | tf_op jit(solution)/shard_map/ppermute | solution.py:17
  98.6 14.8 %collective-permute-start.21 = (bf16[128,1152]{1,0:T(8,128)(2,1)S(1)}, bf16[128,1152]{1,0:T(8,128)(2,1)S(1)}, u32[]{:S(2)}, u32[]{:S(2)}) collective-permute-start(bf16[128,1152]{1,0:T(8,128)(2,1)S(1)} %slice.486), channel_id=1, source_target_pairs={{0,16},{8,24},{16,0},{24,8},{1,17},{9,25},{17,1},{25,9},{2,18},{10... | collective-permute-start | bytes 884744 | tf_op jit(solution)/shard_map/ppermute | solution.py:17
  101.4 13.1 %collective-permute-start.22 = (bf16[128,1152]{1,0:T(8,128)(2,1)S(1)}, bf16[128,1152]{1,0:T(8,128)(2,1)S(1)}, u32[]{:S(2)}, u32[]{:S(2)}) collective-permute-start(bf16[128,1152]{1,0:T(8,128)(2,1)S(1)} %slice.487), channel_id=1, source_target_pairs={{0,8},{8,0},{16,24},{24,16},{1,9},{9,1},{17,25},{25,17},{2,10},{10... | collective-permute-start | bytes 884744 | tf_op jit(solution)/shard_map/ppermute | solution.py:17
  120.5 11.8 %collective-permute-start.13 = (bf16[256,1152]{1,0:T(8,128)(2,1)S(1)}, bf16[256,1152]{1,0:T(8,128)(2,1)S(1)}, u32[]{:S(2)}, u32[]{:S(2)}) collective-permute-start(bf16[256,1152]{1,0:T(8,128)(2,1)S(1)} %get-tuple-element.106), channel_id=1, source_target_pairs={{0,16},{8,24},{16,0},{24,8},{1,17},{9,25},{17,1},{25,9},{2,18},{10... | collective-permute-start | bytes 1769480 | tf_op jit(solution)/shard_map/ppermute | solution.py:17
  120.9 14.5 %collective-permute-start.11 = (bf16[256,1152]{1,0:T(8,128)(2,1)S(1)}, bf16[256,1152]{1,0:T(8,128)(2,1)S(1)}, u32[]{:S(2)}, u32[]{:S(2)}) collective-permute-start(bf16[256,1152]{1,0:T(8,128)(2,1)S(1)} %get-tuple-element.106), channel_id=1, source_target_pairs={{0,8},{8,0},{16,24},{24,16},{1,9},{9,1},{17,25},{25,17},{2,10},{10... | collective-permute-start | bytes 1769480 | tf_op jit(solution)/shard_map/ppermute | solution.py:17
  132.3 9.8 %collective-permute-start.14 = (bf16[128,1152]{1,0:T(8,128)(2,1)S(1)}, bf16[128,1152]{1,0:T(8,128)(2,1)S(1)}, u32[]{:S(2)}, u32[]{:S(2)}) collective-permute-start(bf16[128,1152]{1,0:T(8,128)(2,1)S(1)} %slice.477), channel_id=1, source_target_pairs={{0,8},{8,0},{16,24},{24,16},{1,9},{9,1},{17,25},{25,17},{2,10},{10... | collective-permute-start | bytes 884744 | tf_op jit(solution)/shard_map/ppermute | solution.py:17
  147.6 16.9 %collective-permute-start.23 = (bf16[128,1152]{1,0:T(8,128)(2,1)S(1)}, bf16[128,1152]{1,0:T(8,128)(2,1)S(1)}, u32[]{:S(2)}, u32[]{:S(2)}) collective-permute-start(bf16[128,1152]{1,0:T(8,128)(2,1)S(1)} %get-tuple-element.165), channel_id=1, source_target_pairs={{0,16},{8,24},{16,0},{24,8},{1,17},{9,25},{17,1},{25,9},{2,18},{10... | collective-permute-start | bytes 884744 | tf_op jit(solution)/shard_map/ppermute | solution.py:17
  148.9 15.3 %collective-permute-start.25 = (bf16[128,1152]{1,0:T(8,128)(2,1)S(1)}, bf16[128,1152]{1,0:T(8,128)(2,1)S(1)}, u32[]{:S(2)}, u32[]{:S(2)}) collective-permute-start(bf16[128,1152]{1,0:T(8,128)(2,1)S(1)} %get-tuple-element.166), channel_id=1, source_target_pairs={{0,8},{8,0},{16,24},{24,16},{1,9},{9,1},{17,25},{25,17},{2,10},{10... | collective-permute-start | bytes 884744 | tf_op jit(solution)/shard_map/ppermute | solution.py:17
  151.4 11.4 %collective-permute-start.15 = (bf16[128,1152]{1,0:T(8,128)(2,1)S(1)}, bf16[128,1152]{1,0:T(8,128)(2,1)S(1)}, u32[]{:S(2)}, u32[]{:S(2)}) collective-permute-start(bf16[128,1152]{1,0:T(8,128)(2,1)S(1)} %get-tuple-element.171), channel_id=1, source_target_pairs={{0,16},{8,24},{16,0},{24,8},{1,17},{9,25},{17,1},{25,9},{2,18},{10... | collective-permute-start | bytes 884744 | tf_op jit(solution)/shard_map/ppermute | solution.py:17
  159.8 17.2 %collective-permute-start.18 = (bf16[256,1152]{1,0:T(8,128)(2,1)S(1)}, bf16[256,1152]{1,0:T(8,128)(2,1)S(1)}, u32[]{:S(2)}, u32[]{:S(2)}) collective-permute-start(bf16[256,1152]{1,0:T(8,128)(2,1)S(1)} %pad_maximum_fusion.9), channel_id=1, source_target_pairs={{0,16},{8,24},{16,0},{24,8},{1,17},{9,25},{17,1},{25,9},{2,18},{10... | collective-permute-start | bytes 1769480 | tf_op jit(solution)/shard_map/ppermute | solution.py:17
  163.1 15.6 %collective-permute-start.16 = (bf16[256,1152]{1,0:T(8,128)(2,1)S(1)}, bf16[256,1152]{1,0:T(8,128)(2,1)S(1)}, u32[]{:S(2)}, u32[]{:S(2)}) collective-permute-start(bf16[256,1152]{1,0:T(8,128)(2,1)S(1)} %pad_maximum_fusion.8), channel_id=1, source_target_pairs={{0,8},{8,0},{16,24},{24,16},{1,9},{9,1},{17,25},{25,17},{2,10},{10... | collective-permute-start | bytes 1769480 | tf_op jit(solution)/shard_map/ppermute | solution.py:17
  164.4 20.5 %collective-permute-start.26 = (bf16[256,1152]{1,0:T(8,128)(2,1)S(1)}, bf16[256,1152]{1,0:T(8,128)(2,1)S(1)}, u32[]{:S(2)}, u32[]{:S(2)}) collective-permute-start(bf16[256,1152]{1,0:T(8,128)(2,1)S(1)} %pad_maximum_fusion.11), channel_id=1, source_target_pairs={{0,16},{8,24},{16,0},{24,8},{1,17},{9,25},{17,1},{25,9},{2,18},{10... | collective-permute-start | bytes 1769480 | tf_op jit(solution)/shard_map/ppermute | solution.py:17
  164.6 20.4 %collective-permute-start.24 = (bf16[256,1152]{1,0:T(8,128)(2,1)S(1)}, bf16[256,1152]{1,0:T(8,128)(2,1)S(1)}, u32[]{:S(2)}, u32[]{:S(2)}) collective-permute-start(bf16[256,1152]{1,0:T(8,128)(2,1)S(1)} %pad_maximum_fusion.10), channel_id=1, source_target_pairs={{0,8},{8,0},{16,24},{24,16},{1,9},{9,1},{17,25},{25,17},{2,10},{10... | collective-permute-start | bytes 1769480 | tf_op jit(solution)/shard_map/ppermute | solution.py:17
  190.7 12.5 %collective-permute-start.28 = (bf16[256,1152]{1,0:T(8,128)(2,1)S(1)}, bf16[256,1152]{1,0:T(8,128)(2,1)S(1)}, u32[]{:S(2)}, u32[]{:S(2)}) collective-permute-start(bf16[256,1152]{1,0:T(8,128)(2,1)S(1)} %get-tuple-element.111), channel_id=1, source_target_pairs={{0,16},{8,24},{16,0},{24,8},{1,17},{9,25},{17,1},{25,9},{2,18},{10... | collective-permute-start | bytes 1769480 | tf_op jit(solution)/shard_map/ppermute | solution.py:17
  192.3 13.0 %collective-permute-start.27 = (bf16[256,1152]{1,0:T(8,128)(2,1)S(1)}, bf16[256,1152]{1,0:T(8,128)(2,1)S(1)}, u32[]{:S(2)}, u32[]{:S(2)}) collective-permute-start(bf16[256,1152]{1,0:T(8,128)(2,1)S(1)} %get-tuple-element.111), channel_id=1, source_target_pairs={{0,8},{8,0},{16,24},{24,16},{1,9},{9,1},{17,25},{25,17},{2,10},{10... | collective-permute-start | bytes 1769480 | tf_op jit(solution)/shard_map/ppermute | solution.py:17
  203.3 9.0 %collective-permute-start.30 = (bf16[128,1152]{1,0:T(8,128)(2,1)S(1)}, bf16[128,1152]{1,0:T(8,128)(2,1)S(1)}, u32[]{:S(2)}, u32[]{:S(2)}) collective-permute-start(bf16[128,1152]{1,0:T(8,128)(2,1)S(1)} %slice.499), channel_id=1, source_target_pairs={{0,8},{8,0},{16,24},{24,16},{1,9},{9,1},{17,25},{25,17},{2,10},{10... | collective-permute-start | bytes 884744 | tf_op jit(solution)/shard_map/ppermute | solution.py:17
  258.1 12.2 %collective-permute-start.31 = (bf16[128,1152]{1,0:T(8,128)(2,1)S(1)}, bf16[128,1152]{1,0:T(8,128)(2,1)S(1)}, u32[]{:S(2)}, u32[]{:S(2)}) collective-permute-start(bf16[128,1152]{1,0:T(8,128)(2,1)S(1)} %get-tuple-element.159), channel_id=1, source_target_pairs={{0,16},{8,24},{16,0},{24,8},{1,17},{9,25},{17,1},{25,9},{2,18},{10... | collective-permute-start | bytes 884744 | tf_op jit(solution)/shard_map/ppermute | solution.py:17
  259.0 9.9 %collective-permute-start.33 = (bf16[128,1152]{1,0:T(8,128)(2,1)S(1)}, bf16[128,1152]{1,0:T(8,128)(2,1)S(1)}, u32[]{:S(2)}, u32[]{:S(2)}) collective-permute-start(bf16[128,1152]{1,0:T(8,128)(2,1)S(1)} %get-tuple-element.160), channel_id=1, source_target_pairs={{0,8},{8,0},{16,24},{24,16},{1,9},{9,1},{17,25},{25,17},{2,10},{10... | collective-permute-start | bytes 884744 | tf_op jit(solution)/shard_map/ppermute | solution.py:17
  269.1 9.9 %collective-permute-start.34 = (bf16[256,1152]{1,0:T(8,128)(2,1)S(1)}, bf16[256,1152]{1,0:T(8,128)(2,1)S(1)}, u32[]{:S(2)}, u32[]{:S(2)}) collective-permute-start(bf16[256,1152]{1,0:T(8,128)(2,1)S(1)} %pad_maximum_fusion.13), channel_id=1, source_target_pairs={{0,16},{8,24},{16,0},{24,8},{1,17},{9,25},{17,1},{25,9},{2,18},{10... | collective-permute-start | bytes 1769480 | tf_op jit(solution)/shard_map/ppermute | solution.py:17
  270.5 9.9 %collective-permute-start.32 = (bf16[256,1152]{1,0:T(8,128)(2,1)S(1)}, bf16[256,1152]{1,0:T(8,128)(2,1)S(1)}, u32[]{:S(2)}, u32[]{:S(2)}) collective-permute-start(bf16[256,1152]{1,0:T(8,128)(2,1)S(1)} %pad_maximum_fusion.12), channel_id=1, source_target_pairs={{0,8},{8,0},{16,24},{24,16},{1,9},{9,1},{17,25},{25,17},{2,10},{10... | collective-permute-start | bytes 1769480 | tf_op jit(solution)/shard_map/ppermute | solution.py:17
  294.6 102.8 %reduce-scatter.5.cloned.1.call-start = ((), (), s32[]{:S(2)}) async-start(), calls=%async_computation.2 | async-start | bytes 5971968 | tf_op jit(solution)/shard_map/reduce_scatter | solution.py:228
  344.3 9.5 %collective-permute-start.44 = (f32[2,13,288]{2,1,0:T(8,128)S(1)}, f32[2,13,288]{2,1,0:T(8,128)S(1)}, u32[]{:S(2)}, u32[]{:S(2)}) collective-permute-start(f32[2,13,288]{2,1,0:T(8,128)S(1)} %maximum_select_fusion.1), channel_id=1, source_target_pairs={{0,4},{1,5},{2,6},{3,7},{4,0},{5,1},{6,2},{7,3},{8,12},{9,13},{10,... | collective-permute-start | bytes 89864 | tf_op jit(solution)/shard_map/ppermute | solution.py:42
  (150 other events, 1109.0 us)
Sparse Core Ops, SparseCore 0:
  294.7 37.5 reduce-scatter.6
  334.6 62.8 reduce-scatter.4
